TPU v7x, 128 devices: a whole 4x4x4 slice. The times are simulated.
128 devices in a mesh: row: 16 (over y, z), col: 8 (over x, core).
Axes of the slice: x: 4, y: 4, z: 4, core: 2. Of those that a mesh axis runs over, the one named last changes fastest.
Arguments:
- tokens: bfloat16 [8192, 6144], P('row', 'col'), may hold values from -6 to 6
- weight: bfloat16 [6144, 12288], P('row', 'col'), may hold values from -0.078125 to 0.078125
- cotangent: bfloat16 [8192, 12288], P('row', 'col'), may hold values from -6 to 6
Outputs:
- activated: bfloat16 [8192, 12288], P('row', 'col')
- input_grad: bfloat16 [8192, 6144], P('row', 'col')
All inputs are finite; a program needn't handle non-finite values.
Results may differ from a plain program's by a relative error of at most 0.017.
Values may be sent and summed in bfloat16 or wider, within the bound.
A program may use at most 128 MiB of HBM per device.

v0:
```python
import math

import jax
import jax.numpy as jnp
from jax import lax
from jax.sharding import PartitionSpec as P


def gelu_parts(pre):
    cdf = 0.5 * (1.0 + jax.scipy.special.erf(pre / math.sqrt(2.0)))
    pdf = jnp.exp(-0.5 * pre * pre) / math.sqrt(2.0 * math.pi)
    return (pre * cdf, cdf + pre * pdf)


def local(tokens, weight, cotangent):
    whole = lax.all_gather(tokens, "col", axis=1, tiled=True)
    piece = lax.all_gather(weight, "row", axis=0, tiled=True)
    total = jnp.dot(whole, piece, preferred_element_type=jnp.float32)
    value, slope = gelu_parts(total)
    activated = value.astype(jnp.bfloat16)
    grad_pre = (cotangent.astype(jnp.float32) * slope).astype(jnp.bfloat16)
    partial_sum = lax.dot_general(
        grad_pre, piece, (((1,), (1,)), ((), ())), preferred_element_type=jnp.float32
    )
    summed = lax.psum_scatter(
        partial_sum.astype(jnp.bfloat16), "col", scatter_dimension=1, tiled=True
    )
    return (activated, summed)


def solution(mesh):
    in_specs = (P("row", "col"), P("row", "col"), P("row", "col"))
    out_specs = (P("row", "col"), P("row", "col"))
    return jax.shard_map(local, mesh=mesh, in_specs=in_specs, out_specs=out_specs, check_vma=False)
```

profile of v0, /device:TPU:1, one launch (start us, length us, event | category | flops | bytes accessed | tf_op | source)
XLA Modules:
  0.0 261.1 jit_solution(13074413940239556843)
XLA Ops:
  7.2 0.0 all-gather.3.cloned.1.call-start
  7.2 0.7 all-gather.3.cloned.1.call-update
  7.9 0.0 all-gather.5.cloned.1.call-start
  7.9 0.7 all-gather.5.cloned.1.call-update
  8.6 0.0 copy-start
  8.7 0.0 reduce-scatter.2.cloned.1.call-start
  8.7 45.5 %all-gather.3.cloned.1.call-done = bf16[512,6144]{1,0:T(8,128)(2,1)} async-done(((bf16[512,768]{1,0:T(8,128)(2,1)}), bf16[512,6144]{1,0:T(8,128)(2,1)}) %all-gather.3.cloned.1.call-update) | async-done | bytes 6291472 | tf_op jit(solution)/shard_map/all_gather | solution.py:16
  54.2 124.0 %all-gather.5.cloned.1.call-done = bf16[6144,1536]{1,0:T(8,128)(2,1)} async-done(((bf16[384,1536]{1,0:T(8,128)(2,1)}), bf16[6144,1536]{1,0:T(8,128)(2,1)}) %all-gather.5.cloned.1.call-update) | async-done | bytes 18874384 | tf_op jit(solution)/shard_map/all_gather | solution.py:17
  178.3 17.0 %multiply_convert_fusion = (bf16[512,1536]{1,0:T(8,128)(2,1)}, f32[512,1536]{1,0:T(8,128)}) fusion(bf16[512,6144]{1,0:T(8,128)(2,1)} %all-gather.3.cloned.1.call-done, bf16[6144,1536]{1,0:T(8,128)(2,1)} %all-gather.5.cloned.1.call-done), kind=kOutput, calls=%fused_computation.8 | convolution fusion | flops 9667608576 | bytes 29884416 | tf_op jit(solution)/shard_map/dot_general | solution.py:18
  195.3 0.0 copy-done
  195.3 17.7 %convolution_convert_fusion = bf16[512,6144]{1,0:T(8,128)(2,1)} fusion(bf16[6144,1536]{1,0:T(8,128)(2,1)} %all-gather.5.cloned.1.call-done, f32[512,1536]{1,0:T(8,128)} %get-tuple-element.3, bf16[512,1536]{1,0:T(8,128)(2,1)S(1)} %copy-done), kind=kOutput, calls=%fused_computation | convolution fusion | flops 9675472896 | bytes 29884416 | tf_op jit(solution)/shard_map/dot_general | solution.py:22
  212.9 0.0 reduce-scatter.2.cloned.1.call-update
  213.0 41.6 %reduce-scatter.2.cloned.1.call-done = bf16[512,768]{1,0:T(8,128)(2,1)} async-done(((bf16[512,6144]{1,0:T(8,128)(2,1)}), bf16[512,768]{1,0:T(8,128)(2,1)}) %reduce-scatter.2.cloned.1.call-update) | async-done | bytes 786448 | tf_op jit(solution)/shard_map/reduce_scatter | solution.py:25
Async XLA Ops:
  7.2 47.1 %all-gather.3.cloned.1.call-start = ((), (), s32[]{:S(2)}) async-start(), calls=%async_computation.1 | async-start | bytes 7077888 | tf_op jit(solution)/shard_map/all_gather | solution.py:16
  7.9 170.4 %all-gather.5.cloned.1.call-start = ((), (), s32[]{:S(2)}) async-start(), calls=%async_computation.2 | async-start | bytes 20054016 | tf_op jit(solution)/shard_map/all_gather | solution.py:17
  8.6 186.6 %copy-start = (bf16[512,1536]{1,0:T(8,128)(2,1)S(1)}, bf16[512,1536]{1,0:T(8,128)(2,1)}, u32[]{:S(2)}) copy-start(bf16[512,1536]{1,0:T(8,128)(2,1)} %param.5) | copy-start | bytes 4718596
  8.7 246.0 %reduce-scatter.2.cloned.1.call-start = ((), (), s32[]{:S(2)}) async-start(), calls=%async_computation.3 | async-start | bytes 7077888 | tf_op jit(solution)/shard_map/reduce_scatter | solution.py:25
Sparse Core Ops, SparseCore 0:
  9.7 44.4 all-gather.2
  56.4 121.8 all-gather.4
  213.1 41.4 reduce-scatter.1
where the time goes:
time: 261 us
  waiting for transfers between devices  213 us (82%)
  matrix products  34.7 us (13%)
  between operations  13.7 us (5%)
    all_gather x1, waiting for transfers between devices, local(): piece = lax.all_gather(weight, 'row', axis=0, tiled=True)  124 us
    all_gather x1, waiting for transfers between devices, local(): whole = lax.all_gather(tokens, 'col', axis=1, tiled=True)  45.5 us
    reduce_scatter x1, waiting for transfers between devices, local(): lax.psum_scatter(partial_sum.astype(jnp.bfloat16), 'col', scatter_dimensi...  41.6 us
    dot_general x1, matrix products, local(): lax.dot_general(grad_pre, piece, (((1,), (1,)), ((), ())), preferred_elem...  17.7 us
    dot_general x1, matrix products, local(): total = jnp.dot(whole, piece, preferred_element_type=jnp.float32)  17 us
  transfers between devices with their start and end apart: 3, of which 3 were waited for; matrix products, arithmetic and copies ran while one was open for 0% of the time, Pallas kernels for 0%

commit v1 on v0

v1 whole, which is shorter than its diff:
```python
import functools
import math

import jax
import jax.numpy as jnp
from jax import lax
from jax.experimental import pallas as pl
from jax.experimental.pallas import tpu as pltpu
from jax.sharding import PartitionSpec as P

MESH = pl.DeviceIdType.MESH
RING = 4
CORES = 2
CHUNK = 256


def gelu_parts(pre):
    cdf = 0.5 * (1.0 + lax.erf(pre * (1.0 / math.sqrt(2.0))))
    pdf = jnp.exp(-0.5 * pre * pre) * (1.0 / math.sqrt(2.0 * math.pi))
    return (pre * cdf, cdf + pre * pdf)


def kernel(
    tok_hbm, w_hbm, cot_hbm, act_hbm, grad_hbm,
    tok, w, cot, act, gp, part_out, part_in, staged, first_in, last_in, own, total,
    load_sem, store_sem, w_send, w_recv, t_send, t_recv, d_send, d_recv, x_send, x_recv,
):
    rows, feats = tok_hbm.shape
    depth, width = w_hbm.shape
    chunks = width // CHUNK
    fam = depth // 2
    half = fam // 2
    mid = rows // 2

    r, c = lax.axis_index("row"), lax.axis_index("col")
    y, z = lax.div(r, RING), lax.rem(r, RING)
    x, k = lax.div(c, CORES), lax.rem(c, CORES)

    def at(y, z, x, k):
        return (lax.rem(y, RING) * RING + lax.rem(z, RING), lax.rem(x, RING) * CORES + k)

    neighbours = [
        at(y + 1, z, x, k), at(y + 3, z, x, k), at(y, z + 1, x, k), at(y, z + 3, x, k),
        at(y, z, x + 1, k), at(y, z, x + 3, k), at(y, z, x, 1 - k),
    ]
    x_up, x_down, twin = neighbours[4:]

    def send(src, dst, ssem, rsem, device):
        pltpu.make_async_remote_copy(
            src_ref=src, dst_ref=dst, send_sem=ssem, recv_sem=rsem, device_id=device, device_id_type=MESH
        ).start()

    def arrived(dst, ssem, rsem):
        pltpu.make_async_remote_copy(
            src_ref=dst, dst_ref=dst, send_sem=ssem, recv_sem=rsem, device_id=twin, device_id_type=MESH
        ).wait_recv()

    def sent(src, ssem, rsem):
        pltpu.make_async_remote_copy(
            src_ref=src, dst_ref=src, send_sem=ssem, recv_sem=rsem, device_id=twin, device_id_type=MESH
        ).wait_send()

    def tok_at(x, k, row=0, size=rows):
        return tok.at[pl.ds(row, size), pl.ds(pl.multiple_of((lax.rem(x, RING) * CORES + k) * feats, 128), feats)]

    w_load = pltpu.make_async_copy(w_hbm, w.at[pl.ds(pl.multiple_of(r * depth, 16), depth)], load_sem.at[0])
    w_load.start()
    t_load = pltpu.make_async_copy(tok_hbm, tok_at(x, k), load_sem.at[1])
    t_load.start()
    c_load = pltpu.make_async_copy(cot_hbm, cot, load_sem.at[2])
    c_load.start()

    barrier = pltpu.get_barrier_semaphore()
    for device in neighbours:
        pl.semaphore_signal(barrier, inc=1, device_id=device, device_id_type=MESH)
    pl.semaphore_wait(barrier, len(neighbours))
    w_load.wait()
    t_load.wait()

    def unit(f, p, q, ch, row=0, size=fam):
        ry, rz = (p, q) if f == 0 else (q, p)
        block = lax.rem(ry, RING) * RING + lax.rem(rz, RING)
        return w.at[
            pl.ds(pl.multiple_of(block * depth + f * fam + row, 16), size),
            pl.ds(pl.multiple_of(ch * CHUNK, 128), CHUNK),
        ]

    def family(f):
        if f == 0:
            return y, z, neighbours[0:2], neighbours[2:4]
        return z, y, neighbours[2:4], neighbours[0:2]

    def push(f, ref, ch, index, device):
        send(ref, ref, w_send, w_recv.at[ch, f, index], device)

    def landed(f, ref, ch, index):
        arrived(ref, w_send, w_recv.at[ch, f, index])

    def stage0(ch):
        for f in range(2):
            p, q, ps, qs = family(f)
            for way in range(2):
                push(f, unit(f, p, q, ch), ch, way, ps[way])
        for f in range(2):
            p, q, ps, qs = family(f)
            for way in range(2):
                push(f, unit(f, p, q, ch), ch, 4 + way, qs[way])

    def pass_on(f, ch, j, p):
        _, q, _, qs = family(f)
        for way, step in ((0, -1), (1, 1)):
            landed(f, unit(f, p, q + step + RING, ch), ch, 4 + 2 * j + way)
            push(f, unit(f, p, q + step + RING, ch, way * half, half), ch, 12 + 2 * j + way, qs[way])

    def stage1(ch):
        for f in range(2):
            p, q, ps, qs = family(f)
            for way, step in ((0, -1), (1, 1)):
                there = p + step + RING
                landed(f, unit(f, there, q, ch), ch, way)
                push(f, unit(f, there, q, ch, way * half, half), ch, 2 + way, ps[way])
        for f in range(2):
            p, q, ps, qs = family(f)
            for way, step in ((0, -1), (1, 1)):
                there = p + step + RING
                for way2 in range(2):
                    push(f, unit(f, there, q, ch), ch, 4 + 2 * (1 + way) + way2, qs[way2])
        for f in range(2):
            pass_on(f, ch, 0, family(f)[0])

    def stage2(ch):
        for f in range(2):
            p, q, ps, qs = family(f)
            for way in range(2):
                landed(f, unit(f, p + 2, q, ch, way * half, half), ch, 2 + way)
            for way2 in range(2):
                push(f, unit(f, p + 2, q, ch), ch, 4 + 6 + way2, qs[way2])
        for f in range(2):
            p = family(f)[0]
            pass_on(f, ch, 1, p + 3)
            pass_on(f, ch, 2, p + 1)

    def stage3(ch):
        for f in range(2):
            pass_on(f, ch, 3, family(f)[0] + 2)

    def stage4(ch):
        for f in range(2):
            p, q, ps, qs = family(f)
            for j, there in enumerate((p, p + 3, p + 1, p + 2)):
                for way in range(2):
                    landed(f, unit(f, there, q + 2, ch, way * half, half), ch, 12 + 2 * j + way)

    def tokens0():
        send(tok_at(x, k), tok_at(x, k), t_send, t_recv.at[0], x_up)
        send(tok_at(x, k), tok_at(x, k), t_send, t_recv.at[1], x_down)
        send(tok_at(x, k), tok_at(x, k), t_send, t_recv.at[4], twin)

    def tokens1():
        for way, there, device in ((0, x + 3, x_up), (1, x + 1, x_down)):
            arrived(tok_at(there, k), t_send, t_recv.at[way])
            piece = tok_at(there, k, way * mid, mid)
            send(piece, piece, t_send, t_recv.at[2 + way], device)
            send(tok_at(there, k), tok_at(there, k), t_send, t_recv.at[5 + way], twin)

    def tokens2():
        for way in range(2):
            arrived(tok_at(x + 2, k, way * mid, mid), t_send, t_recv.at[2 + way])
        send(tok_at(x + 2, k), tok_at(x + 2, k), t_send, t_recv.at[7], twin)

    def tokens3():
        for j, there in enumerate((x, x + 3, x + 1, x + 2)):
            arrived(tok_at(there, 1 - k), t_send, t_recv.at[4 + j])

    def store(ch):
        columns = pl.ds(pl.multiple_of(ch * CHUNK, 128), CHUNK)
        return pltpu.make_async_copy(act.at[:, columns], act_hbm.at[:, columns], store_sem.at[ch])

    def compute(ch):
        columns = pl.ds(pl.multiple_of(ch * CHUNK, 128), CHUNK)
        step = rows // 2

        def body(i, _):
            these = pl.ds(pl.multiple_of(i * step, 16), step)
            pre = jnp.dot(tok[these, :], w[:, columns], preferred_element_type=jnp.float32)
            value, slope = gelu_parts(pre)
            act[these, columns] = value.astype(jnp.bfloat16)
            gp[these, columns] = (cot[these, columns].astype(jnp.float32) * slope).astype(jnp.bfloat16)
            return 0

        lax.fori_loop(0, 2, body, 0)
        store(ch).start()

    def tick(t, _):
        for lag, stage in ((3, stage3), (2, stage2), (1, stage1), (0, stage0)):
            @pl.when((t >= lag) & (t - lag < chunks))
            def _():
                stage(t - lag)

        for at_tick, stage in ((0, tokens0), (1, tokens1), (2, tokens2), (4, tokens3)):
            @pl.when(t == at_tick)
            def _():
                stage()

        @pl.when(t == 4)
        def _():
            c_load.wait()

        @pl.when(t >= 4)
        def _():
            stage4(t - 4)
            compute(t - 4)

        return 0

    lax.fori_loop(0, chunks + 4, tick, 0)

    sent(tok.at[:, pl.ds(0, (2 * RING - 1) * feats)], t_send, t_send)

    steps = ((2, 0), (2, 1), (1, 1), (3, 0), (1, 0), (3, 1), (0, 0), (0, 1))

    def product(dx, h, core, dst):
        tile = 256

        def body(n, _):
            start = (lax.rem(x + dx, RING) * CORES + core) * feats + n * tile
            part = lax.dot_general(
                gp[pl.ds(h * mid, mid), :],
                w[pl.ds(pl.multiple_of(start, 128), tile), :],
                (((1,), (1,)), ((), ())),
                preferred_element_type=jnp.float32,
            )
            dst[:, pl.ds(pl.multiple_of(n * tile, 128), tile)] = part.astype(dst.dtype)
            return 0

        lax.fori_loop(0, feats // tile, body, 0)

    def for_twin(s):
        dx, h = steps[s]
        product(dx, h, 1 - k, part_out.at[s])
        send(part_out.at[s], part_in.at[s], d_send.at[s], d_recv.at[s], twin)

    for_twin(0)
    for s, (dx, h) in enumerate(steps):
        if s + 1 < len(steps):
            for_twin(s + 1)
        mine = own.at[pl.ds(h * mid, mid)] if dx == 0 else total
        product(dx, h, k, mine)
        arrived(part_in.at[s], d_send.at[s], d_recv.at[s])
        if dx == 0:
            mine[...] = mine[...] + part_in[s].astype(jnp.float32)
            continue
        summed = mine[...] + part_in[s].astype(jnp.float32)
        if dx == 2:
            staged[s] = summed.astype(jnp.bfloat16)
            send(staged.at[s], first_in.at[h], x_send.at[s], x_recv.at[s], x_up if h == 0 else x_down)
            continue
        way = 0 if dx == 1 else 1
        if h == way:
            arrived(first_in.at[way], x_send.at[way], x_recv.at[way])
            summed = summed + first_in[way].astype(jnp.float32)
        staged[s] = summed.astype(jnp.bfloat16)
        send(staged.at[s], last_in.at[way, h], x_send.at[s], x_recv.at[s], x_up if way == 0 else x_down)

    out_dma = []
    for h in (1, 0):
        s_up = steps.index((1, h))
        s_down = steps.index((3, h))
        arrived(last_in.at[0, h], x_send.at[s_up], x_recv.at[s_up])
        arrived(last_in.at[1, h], x_send.at[s_down], x_recv.at[s_down])
        these = pl.ds(h * mid, mid)
        result = own[these, :] + last_in[0, h].astype(jnp.float32) + last_in[1, h].astype(jnp.float32)
        tok[these, pl.ds(0, feats)] = result.astype(jnp.bfloat16)
        copy = pltpu.make_async_copy(tok.at[these, pl.ds(0, feats)], grad_hbm.at[these, :], load_sem.at[h])
        copy.start()
        out_dma.append(copy)

    for copy in out_dma:
        copy.wait()

    def stored(ch, _):
        store(ch).wait()
        return 0

    lax.fori_loop(0, chunks, stored, 0)
    for s in range(6):
        sent(staged.at[s], x_send.at[s], x_recv.at[s])
    for s in range(8):
        sent(part_out.at[s], d_send.at[s], d_recv.at[s])
    ring = RING * RING - 1
    sent(w.at[pl.ds(0, ring * depth)], w_send, w_send)


def solution(mesh):
    def local(tokens, weight, cotangent):
        rows, feats = tokens.shape
        depth, width = weight.shape
        n_row, n_col = mesh.shape["row"], mesh.shape["col"]
        chunks = width // CHUNK
        mid = rows // 2
        bf16, f32 = jnp.bfloat16, jnp.float32
        dma = pltpu.SemaphoreType.DMA
        return pl.pallas_call(
            kernel,
            out_shape=(
                jax.ShapeDtypeStruct((rows, width), bf16),
                jax.ShapeDtypeStruct((rows, feats), bf16),
            ),
            in_specs=[pl.BlockSpec(memory_space=pl.ANY)] * 3,
            out_specs=(pl.BlockSpec(memory_space=pl.ANY),) * 2,
            scratch_shapes=[
                pltpu.VMEM((rows, feats * n_col), bf16),
                pltpu.VMEM((depth * n_row, width), bf16),
                pltpu.VMEM((rows, width), bf16),
                pltpu.VMEM((rows, width), bf16),
                pltpu.VMEM((rows, width), bf16),
                pltpu.VMEM((8, mid, feats), bf16),
                pltpu.VMEM((8, mid, feats), bf16),
                pltpu.VMEM((6, mid, feats), bf16),
                pltpu.VMEM((2, mid, feats), bf16),
                pltpu.VMEM((2, 2, mid, feats), bf16),
                pltpu.VMEM((rows, feats), f32),
                pltpu.VMEM((mid, feats), f32),
                dma((3,)),
                dma((chunks,)),
                dma,
                dma((chunks, 2, 20)),
                dma,
                dma((8,)),
                dma((8,)),
                dma((8,)),
                dma((6,)),
                dma((6,)),
            ],
            compiler_params=pltpu.CompilerParams(
                collective_id=0, has_side_effects=True, vmem_limit_bytes=60 << 20
            ),
            cost_estimate=pl.CostEstimate(
                flops=4 * rows * feats * n_col * width, bytes_accessed=1 << 24, transcendentals=2 * rows * width
            ),
        )(tokens, weight, cotangent)

    in_specs = (P("row", "col"), P("row", "col"), P("row", "col"))
    out_specs = (P("row", "col"), P("row", "col"))
    return jax.shard_map(local, mesh=mesh, in_specs=in_specs, out_specs=out_specs, check_vma=False)
```

time: 261 us -> 152 us (0.58)
  waiting for transfers between devices: 213 us -> 0 us
  Pallas kernels: 0 us -> 147 us
  matrix products: 34.7 us -> 0 us
  between operations: 13.7 us -> 0.65 us
  local copies, waits for them, and re-layouts: 0.01 us -> 3.61 us
    all_gather x2 -> x0, waiting for transfers between devices: 170 us -> none  [the longest x1 124 us: local(): piece = lax.all_gather(weight, 'row', axis=0, tiled=True)]
    pallas_call x0 -> x1, Pallas kernels: none -> 147 us  [local(): pl.pallas_call(kernel, out_shape=(jax.ShapeDtypeStruct((rows, width), bf1...]
    reduce_scatter x1 -> x0, waiting for transfers between devices: 41.6 us -> none  [local(): lax.psum_scatter(partial_sum.astype(jnp.bfloat16), 'col', scatter_dimensi...]
    dot_general x2 -> x0, matrix products: 34.7 us -> none  [the longest x1 17.7 us: local(): lax.dot_general(grad_pre, piece, (((1,), (1,)), ((), ())), preferred_elem...]
    unnamed x2 -> x4, local copies, waits for them, and re-layouts: 0.01 us -> 3.61 us
  transfers between devices with their start and end apart: 3 -> 0, of which waited for: 3 -> 0; matrix products, arithmetic and copies ran while one was open for 0% -> 0% of each run, Pallas kernels for 0% -> 0%
where the time goes in v1:
time: 152 us; the launch traced here: 151 us
  Pallas kernels  147 us (97%)
  local copies, waits for them, and re-layouts  3.61 us (2%)
    pallas_call x1, Pallas kernels, local(): pl.pallas_call(kernel, out_shape=(jax.ShapeDtypeStruct((rows, width), bf1...  147 us
    unnamed x4, local copies, waits for them, and re-layouts  3.61 us

profile of v1, /device:TPU:1, one launch (start us, length us, event | category | flops | bytes accessed | tf_op | source)
XLA Modules:
  0.0 151.1 jit_solution(4320009903476766907)
XLA Ops:
  0.6 146.9 %shard_map.50 = (bf16[512,1536]{1,0:T(8,128)(2,1)}, bf16[512,768]{1,0:T(8,128)(2,1)}) custom-call(bf16[512,768]{1,0:T(8,128)(2,1)} %tok_hbm.1, bf16[384,1536]{1,0:T(8,128)(2,1)} %w_hbm.1, bf16[512,1536]{1,0:T(8,128)(2,1)} %cot_hbm.1), custom_call_target="tpu_custom_call" | custom-call | flops 19327352832 | bytes 16777216 | tf_op jit(solution)/shard_map/pallas_call | solution.py:303
  147.5 0.0 copy-start
  147.5 2.7 %copy.7 = bf16[512,1536]{1,0:T(8,128)(2,1)} copy(bf16[512,1536]{1,0:T(8,128)(2,1)} %get-tuple-element.4) | data formatting | bytes 3145728
  150.3 0.0 copy-done
  150.3 0.9 copy.8
Async XLA Ops:
  147.5 2.7 %copy-start = (bf16[512,768]{1,0:T(8,128)(2,1)S(1)}, bf16[512,768]{1,0:T(8,128)(2,1)}, u32[]{:S(2)}) copy-start(bf16[512,768]{1,0:T(8,128)(2,1)} %get-tuple-element.5) | copy-start | bytes 2359300

commit v2 on v1

v2 whole, which is shorter than its diff:
```python
import functools
import math

import jax
import jax.numpy as jnp
from jax import lax
from jax.experimental import pallas as pl
from jax.experimental.pallas import tpu as pltpu
from jax.sharding import PartitionSpec as P

MESH = pl.DeviceIdType.MESH
RING = 4
CORES = 2
WIDTHS = (512, 512, 512)
STARTS = tuple(sum(WIDTHS[:i]) for i in range(len(WIDTHS)))
STEPS = ((2, 0), (2, 1), (1, 1), (3, 0), (1, 0), (3, 1), (0, 0), (0, 1))
EARLY = 2
EARLY_CHUNKS, EARLY_TICK = 1, 4

def gelu_parts(pre):
    cdf = 0.5 * (1.0 + lax.erf(pre * (1.0 / math.sqrt(2.0))))
    pdf = jnp.exp(-0.5 * pre * pre) * (1.0 / math.sqrt(2.0 * math.pi))
    return (pre * cdf, cdf + pre * pdf)


def kernel(
    tok_hbm, w_hbm, cot_hbm, act_hbm, grad_hbm,
    tok, ws, cot, pre, act, gp, part_out, part_in, staged, first_in, last_in, begun, own, total,
    load_sem, w_sem, store_sem, w_send, w_recv, t_send, t_recv, d_send, d_recv, x_send, x_recv, g_sem,
):
    rows, feats = tok_hbm.shape
    depth, width = w_hbm.shape
    chunks = len(WIDTHS)
    fam = depth // 2
    half = fam // 2
    mid = rows // 2

    r, c = lax.axis_index("row"), lax.axis_index("col")
    y, z = lax.div(r, RING), lax.rem(r, RING)
    x, k = lax.div(c, CORES), lax.rem(c, CORES)

    def at(y, z, x, k):
        return (lax.rem(y, RING) * RING + lax.rem(z, RING), lax.rem(x, RING) * CORES + k)

    neighbours = [
        at(y + 1, z, x, k), at(y + 3, z, x, k), at(y, z + 1, x, k), at(y, z + 3, x, k),
        at(y, z, x + 1, k), at(y, z, x + 3, k), at(y, z, x, 1 - k),
    ]
    x_up, x_down, twin = neighbours[4:]

    def send(src, dst, ssem, rsem, device):
        pltpu.make_async_remote_copy(
            src_ref=src, dst_ref=dst, send_sem=ssem, recv_sem=rsem, device_id=device, device_id_type=MESH
        ).start()

    def arrived(dst, ssem, rsem):
        pltpu.make_async_remote_copy(
            src_ref=dst, dst_ref=dst, send_sem=ssem, recv_sem=rsem, device_id=twin, device_id_type=MESH
        ).wait_recv()

    def sent(src, ssem, rsem):
        pltpu.make_async_remote_copy(
            src_ref=src, dst_ref=src, send_sem=ssem, recv_sem=rsem, device_id=twin, device_id_type=MESH
        ).wait_send()

    def tok_at(x, k, row=0, size=rows):
        return tok.at[pl.ds(row, size), pl.ds(pl.multiple_of((lax.rem(x, RING) * CORES + k) * feats, 128), feats)]

    def w_load(ch):
        return pltpu.make_async_copy(
            w_hbm.at[:, pl.ds(STARTS[ch], WIDTHS[ch])],
            ws[ch].at[pl.ds(pl.multiple_of(r * depth, 16), depth)],
            w_sem.at[ch],
        )

    for ch in range(chunks):
        w_load(ch).start()
    def t_load():
        return pltpu.make_async_copy(tok_hbm, tok_at(x, k), load_sem.at[1])

    def c_load():
        return pltpu.make_async_copy(cot_hbm, cot, load_sem.at[2])

    t_load().start()
    c_load().start()

    barrier = pltpu.get_barrier_semaphore()
    for device in neighbours:
        pl.semaphore_signal(barrier, inc=1, device_id=device, device_id_type=MESH)
    pl.semaphore_wait(barrier, len(neighbours))

    at_block = [
        [pl.multiple_of((lax.rem(y + dy, RING) * RING + lax.rem(z + dz, RING)) * depth, 16) for dz in range(RING)]
        for dy in range(RING)
    ]
    ring_y, ring_z = neighbours[0:2], neighbours[2:4]

    def unit(f, dp, dq, ch, row=0, size=fam):
        dy, dz = (dp, dq) if f == 0 else (dq, dp)
        return ws[ch].at[pl.ds(at_block[dy % RING][dz % RING] + (f * fam + row), size)]

    def parts(f, ch, n):
        way = n % 2
        back = (-1, 1)[way]
        first, second = (ring_y, ring_z) if f == 0 else (ring_z, ring_y)
        cut = (way * half, half)
        if n < 2:
            return unit(f, 0, 0, ch), unit(f, back, 0, ch), first[way]
        if n < 4:
            return unit(f, back, 0, ch, *cut), unit(f, 2, 0, ch, *cut), first[way]
        place = (0, -1, 1, 2)[(n - 4) % 8 // 2]
        if n < 12:
            return unit(f, place, 0, ch), unit(f, place, back, ch), second[way]
        return unit(f, place, back, ch, *cut), unit(f, place, 2, ch, *cut), second[way]

    def push(f, ch, *ns):
        for n in ns:
            out, _, device = parts(f, ch, n)
            send(out, out, w_send.at[ch], w_recv.at[ch, f, n], device)

    def landed(f, ch, *ns):
        for n in ns:
            arrived(parts(f, ch, n)[1], w_send.at[ch], w_recv.at[ch, f, n])

    def stage0(ch):
        w_load(ch).wait()
        for f in range(2):
            push(f, ch, 0, 1)
        for f in range(2):
            push(f, ch, 4, 5)

    def stage1(f, ch):
        for way in range(2):
            landed(f, ch, way)
            push(f, ch, 2 + way, 6 + 2 * way, 7 + 2 * way)
        for way in range(2):
            landed(f, ch, 4 + way)
            push(f, ch, 12 + way)

    def stage2(f, ch):
        landed(f, ch, 2, 3)
        push(f, ch, 10, 11)
        for n in (6, 7, 8, 9):
            landed(f, ch, n)
            push(f, ch, 8 + n)

    def stage3(f, ch):
        for n in (10, 11):
            landed(f, ch, n)
            push(f, ch, 8 + n)

    ends = ((), (), (12, 13), (14, 15, 16, 17), (18, 19))

    blocks = (
        ((0, 0),),
        ((1, 0), (3, 0), (0, 1), (0, 3)),
        ((2, 0), (0, 2), (1, 1), (1, 3), (3, 1), (3, 3)),
        ((1, 2), (3, 2), (2, 1), (2, 3)),
        ((2, 2),),
    )

    def accumulate(ch, stage):
        columns = pl.ds(STARTS[ch], WIDTHS[ch])
        for f in range(2):
            landed(f, ch, *ends[stage])

        for dy, dz in blocks[stage]:
            there = pl.ds(at_block[dy][dz], depth)

            def body(i, _):
                these = pl.ds(pl.multiple_of(i * mid, 16), mid)
                part = jnp.dot(tok[these, there], ws[ch][there, :], preferred_element_type=jnp.float32)
                pre[these, columns] = part if stage == 0 else pre[these, columns] + part
                return 0

            lax.fori_loop(0, 2, body, 0)

    def tokens0():
        send(tok_at(x, k), tok_at(x, k), t_send, t_recv.at[0], x_up)
        send(tok_at(x, k), tok_at(x, k), t_send, t_recv.at[1], x_down)
        send(tok_at(x, k), tok_at(x, k), t_send, t_recv.at[4], twin)

    def tokens1():
        for way, there, device in ((0, x + 3, x_up), (1, x + 1, x_down)):
            arrived(tok_at(there, k), t_send, t_recv.at[way])
            piece = tok_at(there, k, way * mid, mid)
            send(piece, piece, t_send, t_recv.at[2 + way], device)
            send(tok_at(there, k), tok_at(there, k), t_send, t_recv.at[5 + way], twin)

    def tokens2():
        for way in range(2):
            arrived(tok_at(x + 2, k, way * mid, mid), t_send, t_recv.at[2 + way])
        send(tok_at(x + 2, k), tok_at(x + 2, k), t_send, t_recv.at[7], twin)

    def tokens3():
        for j, there in enumerate((x, x + 3, x + 1, x + 2)):
            arrived(tok_at(there, 1 - k), t_send, t_recv.at[4 + j])

    def store(ch):
        columns = pl.ds(STARTS[ch], WIDTHS[ch])
        return pltpu.make_async_copy(act.at[:, columns], act_hbm.at[:, columns], store_sem.at[ch])

    def activate(ch):
        columns = pl.ds(STARTS[ch], WIDTHS[ch])
        step = rows // 4

        def body(i, _):
            these = pl.ds(pl.multiple_of(i * step, 16), step)
            value, slope = gelu_parts(pre[these, columns])
            act[these, columns] = value.astype(jnp.bfloat16)
            gp[these, columns] = (cot[these, columns].astype(jnp.float32) * slope).astype(jnp.bfloat16)
            return 0

        lax.fori_loop(0, 4, body, 0)
        store(ch).start()

    def product(s, core, dst, chs, begun=None):
        dx, h = STEPS[s]
        tile = 256

        def body(n, _):
            begin = (lax.rem(x + dx, RING) * CORES + core) * feats + n * tile
            columns = pl.ds(pl.multiple_of(n * tile, 128), tile)
            part = 0.0 if begun is None else begun[:, columns]
            for ch in chs:
                part += lax.dot_general(
                    gp[pl.ds(h * mid, mid), pl.ds(STARTS[ch], WIDTHS[ch])],
                    ws[ch][pl.ds(pl.multiple_of(begin, 128), tile), :],
                    (((1,), (1,)), ((), ())),
                    preferred_element_type=jnp.float32,
                )
            dst[:, columns] = part.astype(dst.dtype)
            return 0

        lax.fori_loop(0, feats // tile, body, 0)

    chs = tuple(range(chunks))
    stages = (None, stage1, stage2, stage3)
    behind = []
    stage0(0)
    t_load().wait()
    tokens0()
    if chunks > 1:
        stage0(1)
    behind += [(ch, 0) for ch in range(chunks)]
    for t in range(1, chunks + 4):
        for lag in (3, 2, 1):
            for f in range(2):
                if 0 <= t - lag < chunks:
                    stages[lag](f, t - lag)
        if t + 1 < chunks:
            stage0(t + 1)
        behind += [(t - lag, lag) for lag in (3, 2, 1) if 0 <= t - lag < chunks]
        if t == 1:
            tokens1()
            tokens2()
        if t == 2:
            tokens3()
            c_load().wait()
        if t >= 2:
            for ch, stage in sorted(behind):
                accumulate(ch, stage)
            behind = []
        if t >= 4:
            accumulate(t - 4, 4)
            activate(t - 4)
        if t == EARLY_TICK:
            for n in range(2 * EARLY):
                product(n // 2, (1 - k, k)[n % 2], begun.at[n], chs[:EARLY_CHUNKS])

    sent(tok.at[:, pl.ds(0, (2 * RING - 1) * feats)], t_send, t_send)

    def finish(s, n, core, dst):
        if s < EARLY:
            product(s, core, dst, chs[EARLY_CHUNKS:], begun.at[2 * s + n])
        else:
            product(s, core, dst, chs)

    def for_twin(s):
        finish(s, 0, 1 - k, part_out.at[s])
        send(part_out.at[s], part_in.at[s], d_send.at[s], d_recv.at[s], twin)

    for s in range(EARLY):
        for_twin(s)
    for s, (dx, h) in enumerate(STEPS):
        for later in range(EARLY, 4) if s == 2 else (s + 1,) if s > 2 else ():
            if later < len(STEPS):
                for_twin(later)
        mine = own.at[pl.ds(h * mid, mid)] if dx == 0 else total
        finish(s, 1, k, mine)
        arrived(part_in.at[s], d_send.at[s], d_recv.at[s])
        summed = mine[...] + part_in[s].astype(jnp.float32)
        if dx == 0:
            mine[...] = summed
            continue
        way = h if dx == 2 else dx // 2
        if dx != 2 and h == way:
            arrived(first_in.at[way], x_send.at[way], x_recv.at[way])
            summed = summed + first_in[way].astype(jnp.float32)
        staged[s] = summed.astype(jnp.bfloat16)
        into = first_in.at[h] if dx == 2 else last_in.at[way, h]
        send(staged.at[s], into, x_send.at[s], x_recv.at[s], (x_up, x_down)[way])

    out_dma = []
    for h in range(2):
        for way, dx in enumerate((1, 3)):
            s = STEPS.index((dx, h))
            arrived(last_in.at[way, h], x_send.at[s], x_recv.at[s])
        these = pl.ds(h * mid, mid)
        result = own[these, :] + last_in[0, h].astype(jnp.float32) + last_in[1, h].astype(jnp.float32)
        tok[these, pl.ds(0, feats)] = result.astype(jnp.bfloat16)
        copy = pltpu.make_async_copy(tok.at[these, pl.ds(0, feats)], grad_hbm.at[these, :], g_sem.at[h])
        copy.start()
        out_dma.append(copy)

    for copy in out_dma:
        copy.wait()

    for ch in range(chunks):
        store(ch).wait()
    for s, (dx, _) in enumerate(STEPS):
        sent(part_out.at[s], d_send.at[s], d_recv.at[s])
        if dx:
            sent(staged.at[s], x_send.at[s], x_recv.at[s])
    ring = RING * RING - 1
    for ch in range(chunks):
        sent(ws[ch].at[pl.ds(0, ring * depth)], w_send.at[ch], w_send.at[ch])


def solution(mesh):
    def local(tokens, weight, cotangent):
        rows, feats = tokens.shape
        depth, width = weight.shape
        n_row, n_col = mesh.shape["row"], mesh.shape["col"]
        chunks = len(WIDTHS)
        mid = rows // 2
        bf16, f32 = jnp.bfloat16, jnp.float32
        dma = pltpu.SemaphoreType.DMA
        return pl.pallas_call(
            kernel,
            out_shape=(
                jax.ShapeDtypeStruct((rows, width), bf16),
                jax.ShapeDtypeStruct((rows, feats), bf16),
            ),
            in_specs=[pl.BlockSpec(memory_space=pl.ANY)] * 3,
            out_specs=(pl.BlockSpec(memory_space=pl.ANY),) * 2,
            scratch_shapes=[
                pltpu.VMEM((rows, feats * n_col), bf16),
                tuple(pltpu.VMEM((depth * n_row, size), bf16) for size in WIDTHS),
                pltpu.VMEM((rows, width), bf16),
                pltpu.VMEM((rows, width), f32),
                pltpu.VMEM((rows, width), bf16),
                pltpu.VMEM((rows, width), bf16),
                pltpu.VMEM((8, mid, feats), bf16),
                pltpu.VMEM((8, mid, feats), bf16),
                pltpu.VMEM((6, mid, feats), bf16),
                pltpu.VMEM((2, mid, feats), bf16),
                pltpu.VMEM((2, 2, mid, feats), bf16),
                pltpu.VMEM((2 * EARLY, mid, feats), f32),
                pltpu.VMEM((rows, feats), f32),
                pltpu.VMEM((mid, feats), f32),
                dma((3,)),
                dma((chunks,)),
                dma((chunks,)),
                dma((chunks,)),
                dma((chunks, 2, 20)),
                dma,
                dma((8,)),
                dma((len(STEPS),)),
                dma((len(STEPS),)),
                dma((len(STEPS),)),
                dma((len(STEPS),)),
                dma((2,)),
            ],
            compiler_params=pltpu.CompilerParams(
                collective_id=0, has_side_effects=True, vmem_limit_bytes=60 << 20
            ),
            cost_estimate=pl.CostEstimate(
                flops=4 * rows * feats * n_col * width, bytes_accessed=1 << 24, transcendentals=2 * rows * width
            ),
        )(tokens, weight, cotangent)

    in_specs = (P("row", "col"), P("row", "col"), P("row", "col"))
    out_specs = (P("row", "col"), P("row", "col"))
    return jax.shard_map(local, mesh=mesh, in_specs=in_specs, out_specs=out_specs, check_vma=False)
```

time: 152 us -> 145 us (0.954)
  Pallas kernels: 147 us -> 141 us
    pallas_call x1, Pallas kernels: 147 us -> 141 us  [local(): pl.pallas_call(kernel, out_shape=(jax.ShapeDtypeStruct((rows, width), bf1...]
where the time goes in v2:
time: 145 us
  Pallas kernels  141 us (97%)
  local copies, waits for them, and re-layouts  3.61 us (2%)
    pallas_call x1, Pallas kernels, local(): pl.pallas_call(kernel, out_shape=(jax.ShapeDtypeStruct((rows, width), bf1...  141 us
    unnamed x4, local copies, waits for them, and re-layouts  3.61 us

profile of v2, /device:TPU:1, one launch (start us, length us, event | category | flops | bytes accessed | tf_op | source)
XLA Modules:
  0.0 145.0 jit_solution(15127517893091301690)
XLA Ops:
  0.6 140.7 %shard_map.50 = (bf16[512,1536]{1,0:T(8,128)(2,1)}, bf16[512,768]{1,0:T(8,128)(2,1)}) custom-call(bf16[512,768]{1,0:T(8,128)(2,1)} %tok_hbm.1, bf16[384,1536]{1,0:T(8,128)(2,1)} %w_hbm.1, bf16[512,1536]{1,0:T(8,128)(2,1)} %cot_hbm.1), custom_call_target="tpu_custom_call" | custom-call | flops 19327352832 | bytes 16777216 | tf_op jit(solution)/shard_map/pallas_call | solution.py:339
  141.4 0.0 copy-start
  141.4 2.7 %copy.7 = bf16[512,1536]{1,0:T(8,128)(2,1)} copy(bf16[512,1536]{1,0:T(8,128)(2,1)} %get-tuple-element.4) | data formatting | bytes 3145728
  144.1 0.0 copy-done
  144.1 0.9 copy.8
Async XLA Ops:
  141.4 2.7 %copy-start = (bf16[512,768]{1,0:T(8,128)(2,1)S(1)}, bf16[512,768]{1,0:T(8,128)(2,1)}, u32[]{:S(2)}) copy-start(bf16[512,768]{1,0:T(8,128)(2,1)} %get-tuple-element.5) | copy-start | bytes 2359300

commit v3 on v2

--- a/solution.py
+++ b/solution.py
@@ -24,9 +24,9 @@
 
 
 def kernel(
-    tok_hbm, w_hbm, cot_hbm, act_hbm, grad_hbm,
-    tok, ws, cot, pre, act, gp, part_out, part_in, staged, first_in, last_in, begun, own, total,
-    load_sem, w_sem, store_sem, w_send, w_recv, t_send, t_recv, d_send, d_recv, x_send, x_recv, g_sem,
+    tok_hbm, w_hbm, cot_hbm, act, grad,
+    tok, ws, cot, pre, gp, part_out, part_in, staged, first_in, last_in, begun, own, total,
+    load_sem, w_sem, w_send, w_recv, t_send, t_recv, d_send, d_recv, x_send, x_recv,
 ):
     rows, feats = tok_hbm.shape
     depth, width = w_hbm.shape
@@ -196,11 +196,7 @@
         for j, there in enumerate((x, x + 3, x + 1, x + 2)):
             arrived(tok_at(there, 1 - k), t_send, t_recv.at[4 + j])
 
-    def store(ch):
-        columns = pl.ds(STARTS[ch], WIDTHS[ch])
-        return pltpu.make_async_copy(act.at[:, columns], act_hbm.at[:, columns], store_sem.at[ch])
-
-    def activate(ch):
+    def activate(ch, half_from):
         columns = pl.ds(STARTS[ch], WIDTHS[ch])
         step = rows // 4
 
@@ -211,8 +207,7 @@
             gp[these, columns] = (cot[these, columns].astype(jnp.float32) * slope).astype(jnp.bfloat16)
             return 0
 
-        lax.fori_loop(0, 4, body, 0)
-        store(ch).start()
+        lax.fori_loop(half_from * 2, half_from * 2 + 2, body, 0)
 
     def product(s, core, dst, chs, begun=None):
         dx, h = STEPS[s]
@@ -263,7 +258,9 @@
             behind = []
         if t >= 4:
             accumulate(t - 4, 4)
-            activate(t - 4)
+            if t < chunks + 3:
+                activate(t - 4, 0)
+                activate(t - 4, 1)
         if t == EARLY_TICK:
             for n in range(2 * EARLY):
                 product(n // 2, (1 - k, k)[n % 2], begun.at[n], chs[:EARLY_CHUNKS])
@@ -281,6 +278,7 @@
         send(part_out.at[s], part_in.at[s], d_send.at[s], d_recv.at[s], twin)
 
     for s in range(EARLY):
+        activate(chunks - 1, s)
         for_twin(s)
     for s, (dx, h) in enumerate(STEPS):
         for later in range(EARLY, 4) if s == 2 else (s + 1,) if s > 2 else ():
@@ -301,23 +299,16 @@
         into = first_in.at[h] if dx == 2 else last_in.at[way, h]
         send(staged.at[s], into, x_send.at[s], x_recv.at[s], (x_up, x_down)[way])
 
-    out_dma = []
     for h in range(2):
         for way, dx in enumerate((1, 3)):
             s = STEPS.index((dx, h))
             arrived(last_in.at[way, h], x_send.at[s], x_recv.at[s])
-        these = pl.ds(h * mid, mid)
-        result = own[these, :] + last_in[0, h].astype(jnp.float32) + last_in[1, h].astype(jnp.float32)
-        tok[these, pl.ds(0, feats)] = result.astype(jnp.bfloat16)
-        copy = pltpu.make_async_copy(tok.at[these, pl.ds(0, feats)], grad_hbm.at[these, :], g_sem.at[h])
-        copy.start()
-        out_dma.append(copy)
-
-    for copy in out_dma:
-        copy.wait()
-
-    for ch in range(chunks):
-        store(ch).wait()
+        for i in range(2):
+            size = mid // 2
+            these, inner = pl.ds(h * mid + i * size, size), pl.ds(i * size, size)
+            result = own[these, :] + last_in[0, h, inner].astype(jnp.float32) + last_in[1, h, inner].astype(jnp.float32)
+            grad[these, :] = result.astype(jnp.bfloat16)
+
     for s, (dx, _) in enumerate(STEPS):
         sent(part_out.at[s], d_send.at[s], d_recv.at[s])
         if dx:
@@ -325,6 +316,19 @@
     ring = RING * RING - 1
     for ch in range(chunks):
         sent(ws[ch].at[pl.ds(0, ring * depth)], w_send.at[ch], w_send.at[ch])
+
+
+def hand_on(act_in, grad_in, act_out, grad_out, sem):
+    copies = []
+    for n, (src, dst) in enumerate(((act_in, act_out), (grad_in, grad_out))):
+        size = src.shape[0] // 4
+        for i in range(4):
+            these = pl.ds(i * size, size)
+            copies.append(pltpu.make_async_copy(src.at[these], dst.at[these], sem.at[n, i]))
+    for copy in copies:
+        copy.start()
+    for copy in copies:
+        copy.wait()
 
 
 def solution(mesh):
@@ -336,20 +340,19 @@
         mid = rows // 2
         bf16, f32 = jnp.bfloat16, jnp.float32
         dma = pltpu.SemaphoreType.DMA
-        return pl.pallas_call(
+        results = pl.pallas_call(
             kernel,
             out_shape=(
-                jax.ShapeDtypeStruct((rows, width), bf16),
-                jax.ShapeDtypeStruct((rows, feats), bf16),
+                pltpu.VMEM((rows, width), bf16),
+                pltpu.VMEM((rows, feats), bf16),
             ),
             in_specs=[pl.BlockSpec(memory_space=pl.ANY)] * 3,
-            out_specs=(pl.BlockSpec(memory_space=pl.ANY),) * 2,
+            out_specs=(pl.BlockSpec(memory_space=pltpu.VMEM),) * 2,
             scratch_shapes=[
                 pltpu.VMEM((rows, feats * n_col), bf16),
                 tuple(pltpu.VMEM((depth * n_row, size), bf16) for size in WIDTHS),
                 pltpu.VMEM((rows, width), bf16),
                 pltpu.VMEM((rows, width), f32),
-                pltpu.VMEM((rows, width), bf16),
                 pltpu.VMEM((rows, width), bf16),
                 pltpu.VMEM((8, mid, feats), bf16),
                 pltpu.VMEM((8, mid, feats), bf16),
@@ -362,7 +365,6 @@
                 dma((3,)),
                 dma((chunks,)),
                 dma((chunks,)),
-                dma((chunks,)),
                 dma((chunks, 2, 20)),
                 dma,
                 dma((8,)),
@@ -370,15 +372,22 @@
                 dma((len(STEPS),)),
                 dma((len(STEPS),)),
                 dma((len(STEPS),)),
-                dma((2,)),
             ],
             compiler_params=pltpu.CompilerParams(
-                collective_id=0, has_side_effects=True, vmem_limit_bytes=60 << 20
+                collective_id=0, has_side_effects=True, vmem_limit_bytes=52 << 20
             ),
             cost_estimate=pl.CostEstimate(
                 flops=4 * rows * feats * n_col * width, bytes_accessed=1 << 24, transcendentals=2 * rows * width
             ),
         )(tokens, weight, cotangent)
+        return pl.pallas_call(
+            hand_on,
+            out_shape=tuple(jax.ShapeDtypeStruct(a.shape, a.dtype) for a in results),
+            in_specs=[pl.BlockSpec(memory_space=pltpu.VMEM)] * 2,
+            out_specs=(pl.BlockSpec(memory_space=pl.ANY),) * 2,
+            scratch_shapes=[dma((2, 4))],
+            compiler_params=pltpu.CompilerParams(vmem_limit_bytes=8 << 20),
+        )(*results)
 
     in_specs = (P("row", "col"), P("row", "col"), P("row", "col"))
     out_specs = (P("row", "col"), P("row", "col"))

time: 145 us -> 142 us (0.979)
  local copies, waits for them, and re-layouts: 3.61 us -> 0 us
    unnamed x4 -> x0, local copies, waits for them, and re-layouts: 3.61 us -> none
    pallas_call x1 -> x2, Pallas kernels: 141 us -> 141 us  [the longest x1 140 us: local(): pl.pallas_call(kernel, out_shape=(pltpu.VMEM((rows, width), bf16), pltpu....]
where the time goes in v3:
time: 142 us
  Pallas kernels  141 us (99%)
    pallas_call x1, Pallas kernels, local(): pl.pallas_call(kernel, out_shape=(pltpu.VMEM((rows, width), bf16), pltpu....  140 us

profile of v3, /device:TPU:1, one launch (start us, length us, event | category | flops | bytes accessed | tf_op | source)
XLA Modules:
  0.0 141.9 jit_solution(17364414437584428688)
XLA Ops:
  0.6 139.8 %shard_map.50 = (bf16[512,1536]{1,0:T(8,128)(2,1)S(1)}, bf16[512,768]{1,0:T(8,128)(2,1)S(1)}) custom-call(bf16[512,768]{1,0:T(8,128)(2,1)} %tok_hbm.1, bf16[384,1536]{1,0:T(8,128)(2,1)} %w_hbm.1, bf16[512,1536]{1,0:T(8,128)(2,1)} %cot_hbm.1), custom_call_target="tpu_custom_call" | custom-call | flops 19327352832 | bytes 16777216 | tf_op jit(solution)/shard_map/pallas_call | solution.py:343
  140.4 1.5 %shard_map.51 = (bf16[512,1536]{1,0:T(8,128)(2,1)}, bf16[512,768]{1,0:T(8,128)(2,1)}) custom-call(bf16[512,1536]{1,0:T(8,128)(2,1)S(1)} %get-tuple-element.4.act_in, bf16[512,768]{1,0:T(8,128)(2,1)S(1)} %get-tuple-element.5.grad_in), custom_call_target="tpu_custom_call" | custom-call | tf_op jit(solution)/shard_map/pallas_call | solution.py:383

commit v4 on v3

--- a/solution.py
+++ b/solution.py
@@ -15,7 +15,7 @@
 STARTS = tuple(sum(WIDTHS[:i]) for i in range(len(WIDTHS)))
 STEPS = ((2, 0), (2, 1), (1, 1), (3, 0), (1, 0), (3, 1), (0, 0), (0, 1))
 EARLY = 2
-EARLY_CHUNKS, EARLY_TICK = 1, 4
+EARLY_CHUNKS, EARLY_TICK = 1, 3
 
 def gelu_parts(pre):
     cdf = 0.5 * (1.0 + lax.erf(pre * (1.0 / math.sqrt(2.0))))
@@ -211,7 +211,7 @@
 
     def product(s, core, dst, chs, begun=None):
         dx, h = STEPS[s]
-        tile = 256
+        tile = 256 if begun is None else feats
 
         def body(n, _):
             begin = (lax.rem(x + dx, RING) * CORES + core) * feats + n * tile
@@ -238,7 +238,7 @@
     if chunks > 1:
         stage0(1)
     behind += [(ch, 0) for ch in range(chunks)]
-    for t in range(1, chunks + 4):
+    for t in range(1, chunks + 3):
         for lag in (3, 2, 1):
             for f in range(2):
                 if 0 <= t - lag < chunks:
@@ -256,11 +256,11 @@
             for ch, stage in sorted(behind):
                 accumulate(ch, stage)
             behind = []
-        if t >= 4:
-            accumulate(t - 4, 4)
-            if t < chunks + 3:
-                activate(t - 4, 0)
-                activate(t - 4, 1)
+        if t >= 3:
+            accumulate(t - 3, 4)
+            if t < chunks + 2:
+                activate(t - 3, 0)
+                activate(t - 3, 1)
         if t == EARLY_TICK:
             for n in range(2 * EARLY):
                 product(n // 2, (1 - k, k)[n % 2], begun.at[n], chs[:EARLY_CHUNKS])
@@ -276,6 +276,12 @@
     def for_twin(s):
         finish(s, 0, 1 - k, part_out.at[s])
         send(part_out.at[s], part_in.at[s], d_send.at[s], d_recv.at[s], twin)
+
+    def pieces(s):
+        dx, h = STEPS[s]
+        if dx != 2 and h == dx // 2:
+            return [(pl.ds(i * (mid // 2), mid // 2), s + 2 * i) for i in range(2)]
+        return [(pl.ds(0, mid), s)]
 
     for s in range(EARLY):
         activate(chunks - 1, s)
@@ -296,14 +302,17 @@
             arrived(first_in.at[way], x_send.at[way], x_recv.at[way])
             summed = summed + first_in[way].astype(jnp.float32)
         staged[s] = summed.astype(jnp.bfloat16)
-        into = first_in.at[h] if dx == 2 else last_in.at[way, h]
-        send(staged.at[s], into, x_send.at[s], x_recv.at[s], (x_up, x_down)[way])
-
-    for h in range(2):
-        for way, dx in enumerate((1, 3)):
-            s = STEPS.index((dx, h))
-            arrived(last_in.at[way, h], x_send.at[s], x_recv.at[s])
-        for i in range(2):
+        for piece, sem in pieces(s):
+            into = first_in.at[h] if dx == 2 else last_in.at[way, h, piece]
+            send(staged.at[s, piece], into, x_send.at[sem], x_recv.at[sem], (x_up, x_down)[way])
+
+    for i in range(2):
+        for h in range(2):
+            for way, dx in enumerate((1, 3)):
+                these = pieces(STEPS.index((dx, h)))
+                if i < len(these):
+                    piece, sem = these[i]
+                    arrived(last_in.at[way, h, piece], x_send.at[sem], x_recv.at[sem])
             size = mid // 2
             these, inner = pl.ds(h * mid + i * size, size), pl.ds(i * size, size)
             result = own[these, :] + last_in[0, h, inner].astype(jnp.float32) + last_in[1, h, inner].astype(jnp.float32)
@@ -312,7 +321,8 @@
     for s, (dx, _) in enumerate(STEPS):
         sent(part_out.at[s], d_send.at[s], d_recv.at[s])
         if dx:
-            sent(staged.at[s], x_send.at[s], x_recv.at[s])
+            for piece, sem in pieces(s):
+                sent(staged.at[s, piece], x_send.at[sem], x_recv.at[sem])
     ring = RING * RING - 1
     for ch in range(chunks):
         sent(ws[ch].at[pl.ds(0, ring * depth)], w_send.at[ch], w_send.at[ch])

time: 142 us -> 141 us (level)
    pallas_call x1, Pallas kernels: 140 us -> 138 us  [local(): pl.pallas_call(kernel, out_shape=(pltpu.VMEM((rows, width), bf16), pltpu....]
where the time goes in v4:
time: 141 us; the launch traced here: 140 us
  Pallas kernels  140 us (99%)
    pallas_call x1, Pallas kernels, local(): pl.pallas_call(kernel, out_shape=(pltpu.VMEM((rows, width), bf16), pltpu....  138 us

profile of v4, /device:TPU:1, one launch (start us, length us, event | category | flops | bytes accessed | tf_op | source)
XLA Modules:
  0.0 140.5 jit_solution(5300508506438867404)
XLA Ops:
  0.6 138.2 %shard_map.50 = (bf16[512,1536]{1,0:T(8,128)(2,1)S(1)}, bf16[512,768]{1,0:T(8,128)(2,1)S(1)}) custom-call(bf16[512,768]{1,0:T(8,128)(2,1)} %tok_hbm.1, bf16[384,1536]{1,0:T(8,128)(2,1)} %w_hbm.1, bf16[512,1536]{1,0:T(8,128)(2,1)} %cot_hbm.1), custom_call_target="tpu_custom_call" | custom-call | flops 19327352832 | bytes 16777216 | tf_op jit(solution)/shard_map/pallas_call | solution.py:353
  138.9 1.5 %shard_map.51 = (bf16[512,1536]{1,0:T(8,128)(2,1)}, bf16[512,768]{1,0:T(8,128)(2,1)}) custom-call(bf16[512,1536]{1,0:T(8,128)(2,1)S(1)} %get-tuple-element.4.act_in, bf16[512,768]{1,0:T(8,128)(2,1)S(1)} %get-tuple-element.5.grad_in), custom_call_target="tpu_custom_call" | custom-call | tf_op jit(solution)/shard_map/pallas_call | solution.py:393

commit v5 on v4

--- a/solution.py
+++ b/solution.py
@@ -264,12 +264,15 @@
         if t == EARLY_TICK:
             for n in range(2 * EARLY):
                 product(n // 2, (1 - k, k)[n % 2], begun.at[n], chs[:EARLY_CHUNKS])
+        if t == chunks + 1:
+            for n in range(2 * EARLY):
+                product(n // 2, (1 - k, k)[n % 2], begun.at[n], chs[EARLY_CHUNKS:-1], begun.at[n])
 
     sent(tok.at[:, pl.ds(0, (2 * RING - 1) * feats)], t_send, t_send)
 
     def finish(s, n, core, dst):
         if s < EARLY:
-            product(s, core, dst, chs[EARLY_CHUNKS:], begun.at[2 * s + n])
+            product(s, core, dst, chs[-1:], begun.at[2 * s + n])
         else:
             product(s, core, dst, chs)
 

time: 141 us -> 141 us (level)
  no operation moved by 1% of the time
where the time goes in v5:
time: 141 us
  Pallas kernels  140 us (99%)
    pallas_call x1, Pallas kernels, local(): pl.pallas_call(kernel, out_shape=(pltpu.VMEM((rows, width), bf16), pltpu....  138 us

profile of v5, /device:TPU:1, one launch (start us, length us, event | category | flops | bytes accessed | tf_op | source)
XLA Modules:
  0.0 140.7 jit_solution(11400819647997894792)
XLA Ops:
  0.6 138.5 %shard_map.50 = (bf16[512,1536]{1,0:T(8,128)(2,1)S(1)}, bf16[512,768]{1,0:T(8,128)(2,1)S(1)}) custom-call(bf16[512,768]{1,0:T(8,128)(2,1)} %tok_hbm.1, bf16[384,1536]{1,0:T(8,128)(2,1)} %w_hbm.1, bf16[512,1536]{1,0:T(8,128)(2,1)} %cot_hbm.1), custom_call_target="tpu_custom_call" | custom-call | flops 19327352832 | bytes 16777216 | tf_op jit(solution)/shard_map/pallas_call | solution.py:356
  139.1 1.5 %shard_map.51 = (bf16[512,1536]{1,0:T(8,128)(2,1)}, bf16[512,768]{1,0:T(8,128)(2,1)}) custom-call(bf16[512,1536]{1,0:T(8,128)(2,1)S(1)} %get-tuple-element.4.act_in, bf16[512,768]{1,0:T(8,128)(2,1)S(1)} %get-tuple-element.5.grad_in), custom_call_target="tpu_custom_call" | custom-call | tf_op jit(solution)/shard_map/pallas_call | solution.py:396

commit v6 on v5

--- a/solution.py
+++ b/solution.py
@@ -159,10 +159,11 @@
         ((2, 2),),
     )
 
-    def accumulate(ch, stage):
+    def accumulate(ch, stage, begin=0, end=2):
         columns = pl.ds(STARTS[ch], WIDTHS[ch])
         for f in range(2):
-            landed(f, ch, *ends[stage])
+            if begin == 0:
+                landed(f, ch, *ends[stage])
 
         for dy, dz in blocks[stage]:
             there = pl.ds(at_block[dy][dz], depth)
@@ -173,7 +174,7 @@
                 pre[these, columns] = part if stage == 0 else pre[these, columns] + part
                 return 0
 
-            lax.fori_loop(0, 2, body, 0)
+            lax.fori_loop(begin, end, body, 0)
 
     def tokens0():
         send(tok_at(x, k), tok_at(x, k), t_send, t_recv.at[0], x_up)
@@ -257,7 +258,7 @@
                 accumulate(ch, stage)
             behind = []
         if t >= 3:
-            accumulate(t - 3, 4)
+            accumulate(t - 3, 4, 0, 1 if t == chunks + 2 else 2)
             if t < chunks + 2:
                 activate(t - 3, 0)
                 activate(t - 3, 1)
@@ -287,6 +288,8 @@
         return [(pl.ds(0, mid), s)]
 
     for s in range(EARLY):
+        if s == 1:
+            accumulate(chunks - 1, 4, 1, 2)
         activate(chunks - 1, s)
         for_twin(s)
     for s, (dx, h) in enumerate(STEPS):

time: 141 us -> 140 us (level)
  no operation moved by 1% of the time
where the time goes in v6:
time: 140 us
  Pallas kernels  139 us (99%)
    pallas_call x1, Pallas kernels, local(): pl.pallas_call(kernel, out_shape=(pltpu.VMEM((rows, width), bf16), pltpu....  138 us

profile of v6, /device:TPU:1, one launch (start us, length us, event | category | flops | bytes accessed | tf_op | source)
XLA Modules:
  0.0 140.2 jit_solution(6353591749462744724)
XLA Ops:
  0.6 137.9 %shard_map.50 = (bf16[512,1536]{1,0:T(8,128)(2,1)S(1)}, bf16[512,768]{1,0:T(8,128)(2,1)S(1)}) custom-call(bf16[512,768]{1,0:T(8,128)(2,1)} %tok_hbm.1, bf16[384,1536]{1,0:T(8,128)(2,1)} %w_hbm.1, bf16[512,1536]{1,0:T(8,128)(2,1)} %cot_hbm.1), custom_call_target="tpu_custom_call" | custom-call | flops 19327352832 | bytes 16777216 | tf_op jit(solution)/shard_map/pallas_call | solution.py:359
  138.6 1.5 %shard_map.51 = (bf16[512,1536]{1,0:T(8,128)(2,1)}, bf16[512,768]{1,0:T(8,128)(2,1)}) custom-call(bf16[512,1536]{1,0:T(8,128)(2,1)S(1)} %get-tuple-element.4.act_in, bf16[512,768]{1,0:T(8,128)(2,1)S(1)} %get-tuple-element.5.grad_in), custom_call_target="tpu_custom_call" | custom-call | tf_op jit(solution)/shard_map/pallas_call | solution.py:399
